TPU v7x, 512 devices: a whole 4x4x16 slice. The times are simulated.
512 devices in a mesh: section: 4 (over x), replica: 16 (over z_lo, y), expert: 8 (over z_hi, core).
Axes of the slice: x: 4, y: 4, z: 16 (z_hi: 4, z_lo: 4; z = z_hi * 4 + z_lo), core: 2. Of those that a mesh axis runs over, the one named last changes fastest.
Arguments:
- tokens: bfloat16 [3, 256, 1536], P(None, 'replica'), may hold values from -6 to 6
- attn_gain: float32 [4, 1536], P('section'), may hold values from 0.25 to 1.75
- w_query: bfloat16 [4, 1536, 2048], P('section', None, 'expert'), may hold values from -0.15625 to 0.15625
- w_keyval: bfloat16 [4, 1536, 8, 128], P('section', None, 'expert'), may hold values from -0.15625 to 0.15625
- sinks: float32 [4, 32], P('section', 'expert'), may hold values from -2 to 260
- w_out: bfloat16 [4, 2048, 1536], P('section', 'expert'), may hold values from -0.125 to 0.125
- ffn_gain: float32 [4, 1536], P('section'), may hold values from 0.25 to 1.75
- router: bfloat16 [4, 1536, 16], P('section'), may hold values from -0.15625 to 0.15625
- w_gate_up: bfloat16 [4, 16, 2, 1536, 2048], P('section', 'replica', None, None, 'expert'), may hold values from -0.15625 to 0.15625
- w_down: bfloat16 [4, 16, 2048, 1536], P('section', 'replica', 'expert'), may hold values from -0.125 to 0.125
- kv_pool: bfloat16 [4, 2048, 16, 8, 128], P('section', 'replica', None, 'expert'), may hold values from -6 to 6
- block_table: int32 [256, 8], P('replica'), may hold values from 0 to 127, as said below
- lengths: int32 [256], P('replica'), may hold values from 1 to 128, as said below
- expert_ids: int32 [4, 3, 256, 4], P('section', None, 'replica'), may hold values from 0 to 15, all different within a row; in each aligned block of 16 rows (0 to 15, 16 to 31, ..., all dimensions but the last counted through in order) at most 5 rows name the same one
Outputs:
- layer_out: bfloat16 [4, 3, 256, 1536], P('section', None, 'replica', 'expert')
- fresh_kv: bfloat16 [4, 3, 256, 8, 128], P('section', None, 'replica', 'expert')
Inputs may be any that keep to these rules, and one draw needn't show every extreme that they name: `block_table`: rows 0 to 11 of each replica are its own requests and index its own pool; its last 4 rows are requests taken over from the replica before it (replica 0 from the last one) and index that replica's pool. All blocks named in one pool are different. `lengths`: some request has exactly 128 cached tokens. `expert_ids`: A row names 4 different experts. For each layer and step, at most 5 of one replica's 16 rows name the same expert, and that count is reached.
All inputs are finite; a program needn't handle non-finite values.
Results may differ from a plain program's by a relative error of at most 0.027.
Values may be sent and summed in bfloat16 or wider, within the bound.
A program may use at most 64 MiB of HBM per device.

v0:
```python
import jax
import jax.numpy as jnp
from jax import lax
from jax.sharding import PartitionSpec as P

MIG = 4
EPS = 1e-05
THETA = 150000.0
NEG = -1e30


def shifted(shard, axis, by):
    length = lax.axis_size(axis)
    return lax.ppermute(shard, axis, [(i, (i + by) % length) for i in range(length)])


def shifted_2(value, axis, steps):
    count = lax.axis_size(axis)
    leading, last = (max(0, -steps), min(count, count - steps))
    return lax.ppermute(value, axis, [(source, source + steps) for source in range(leading, last)])


def normed(values, gain):
    wide = values.astype(jnp.float32)
    mean_sq = jnp.mean(wide * wide, axis=-1, keepdims=True)
    return (wide * lax.rsqrt(mean_sq + EPS) * gain).astype(jnp.bfloat16)


def rotated(vectors, places):
    half = vectors.shape[-1] // 2
    freq = THETA ** (-2.0 * jnp.arange(half).astype(jnp.float32) / vectors.shape[-1])
    angle = places.astype(jnp.float32)[:, None] * freq[None, :]
    cosine = jnp.cos(angle)[:, None, :]
    sine = jnp.sin(angle)[:, None, :]
    first = vectors[..., :half]
    second = vectors[..., half:]
    return jnp.concatenate(
        [first * cosine - second * sine, second * cosine + first * sine], axis=-1
    )


def attend(query, cache, live_len, fresh, step_at, sink):
    head_dim = query.shape[-1]
    scale = head_dim ** (-0.5)
    past_keys = cache[..., :head_dim]
    past_vals = cache[..., head_dim:]
    score = (
        jnp.einsum("rkgd,rckd->rkgc", query, past_keys, preferred_element_type=jnp.float32) * scale
    )
    live = jnp.arange(cache.shape[1])[None, :] < live_len[:, None]
    score = jnp.where(live[:, None, None, :], score, NEG)
    new_keys = fresh[..., :head_dim]
    new_vals = fresh[..., head_dim:]
    recent = (
        jnp.einsum("rkgd,srkd->rkgs", query, new_keys, preferred_element_type=jnp.float32) * scale
    )
    seen = jnp.arange(fresh.shape[0]) <= step_at
    recent = jnp.where(seen[None, None, None, :], recent, NEG)
    peak = jnp.maximum(jnp.maximum(jnp.max(score, -1), jnp.max(recent, -1)), sink[None])
    past_w = jnp.exp(score - peak[..., None])
    new_w = jnp.exp(recent - peak[..., None])
    total = jnp.sum(past_w, -1) + jnp.sum(new_w, -1) + jnp.exp(sink[None] - peak)
    past_b = (past_w / total[..., None]).astype(jnp.bfloat16)
    new_b = (new_w / total[..., None]).astype(jnp.bfloat16)
    merged = jnp.einsum("rkgc,rckd->rkgd", past_b, past_vals, preferred_element_type=jnp.float32)
    merged = merged + jnp.einsum(
        "rkgs,srkd->rkgd", new_b, new_vals, preferred_element_type=jnp.float32
    )
    return merged.astype(jnp.bfloat16)


def local(
    tokens,
    attn_gain,
    w_query,
    w_keyval,
    sinks,
    w_out,
    ffn_gain,
    router,
    w_gate_up,
    w_down,
    kv_pool,
    block_table,
    lengths,
    expert_ids,
):
    step_count, row_count, model_width = tokens.shape
    expert_count = router.shape[2]
    kv_local = w_keyval.shape[2]
    pair_width = w_keyval.shape[3]
    head_dim = pair_width // 2
    q_local = sinks.shape[1]
    group = q_local // kv_local
    choose_count = expert_ids.shape[3]
    part_count = lax.axis_size("expert")
    share_width = model_width // part_count
    slot_cap = min(
        row_count, (5 * row_count * choose_count + 4 * expert_count - 1) // (4 * expert_count)
    )
    section_index = lax.axis_index("section")
    lane_index = lax.axis_index("expert")
    section_count = lax.axis_size("section")
    own_pool = kv_pool[0]
    block_count = block_table.shape[1]
    depth = block_count * own_pool.shape[1]
    staying = row_count - MIG
    wanted = shifted(block_table[staying:], "replica", -1)
    leaving = own_pool[wanted.reshape(-1)]
    arrived = shifted(leaving, "replica", 1)
    resident = own_pool[block_table[:staying].reshape(-1)]
    cache = jnp.concatenate([resident, arrived], axis=0).reshape(
        row_count, depth, kv_local, pair_width
    )
    query_weight = w_query[0]
    keyval_weight = w_keyval[0].reshape(model_width, kv_local * pair_width)
    out_weight = w_out[0]
    sink_local = sinks[0].reshape(kv_local, group)
    router_weight = router[0]
    gate_up = w_gate_up[0, 0]
    down_weight = w_down[0, 0]
    expert_range = jnp.arange(expert_count)
    slot_range = jnp.arange(expert_count * slot_cap)
    fresh = jnp.zeros((step_count, row_count, kv_local, pair_width), jnp.bfloat16)
    results = jnp.zeros((step_count, row_count, share_width), jnp.bfloat16)
    incoming = None
    tick_total = step_count + section_count - 1
    for tick_index in range(tick_total):
        offset = tick_index - section_index
        active = (offset >= 0) & (offset < step_count)
        step_at = jnp.clip(offset, 0, step_count - 1)
        first_input = lax.dynamic_index_in_dim(tokens, step_at, 0, keepdims=False)
        if tick_index == 0:
            current = first_input
        else:
            current = jnp.where(section_index == 0, first_input, incoming)
        places = lengths + step_at
        normal_in = normed(current, attn_gain[0])
        query = jnp.dot(normal_in, query_weight, preferred_element_type=jnp.float32).reshape(
            row_count, q_local, head_dim
        )
        query = (
            rotated(query, places)
            .astype(jnp.bfloat16)
            .reshape(row_count, kv_local, group, head_dim)
        )
        keyval = jnp.dot(normal_in, keyval_weight, preferred_element_type=jnp.float32).reshape(
            row_count, kv_local, pair_width
        )
        new_entry = jnp.concatenate(
            [rotated(keyval[..., :head_dim], places), keyval[..., head_dim:]], axis=-1
        ).astype(jnp.bfloat16)
        fresh_now = fresh.at[step_at].set(new_entry)
        attended = attend(query, cache, lengths, fresh_now, step_at, sink_local).reshape(
            row_count, q_local * head_dim
        )
        mixed = lax.psum(
            jnp.dot(attended, out_weight, preferred_element_type=jnp.float32).astype(jnp.bfloat16),
            "expert",
        ).astype(jnp.float32)
        after_attn = (current.astype(jnp.float32) + mixed).astype(jnp.bfloat16)
        mlp_in = normed(after_attn, ffn_gain[0])
        logits = jnp.dot(mlp_in, router_weight, preferred_element_type=jnp.float32)
        chosen = lax.dynamic_index_in_dim(expert_ids[0], step_at, 0, keepdims=False)
        chosen_hot = chosen[:, :, None] == expert_range[None, None, :]
        gates = jax.nn.sigmoid(jnp.sum(jnp.where(chosen_hot, logits[:, None, :], 0.0), -1))
        weight = gates / jnp.sum(gates, -1, keepdims=True)
        flat_hot = chosen_hot.reshape(row_count * choose_count, expert_count).astype(jnp.int32)
        earlier = jnp.cumsum(flat_hot, axis=0) - flat_hot
        slot_of = jnp.sum(earlier * flat_hot, -1)
        target = chosen.reshape(-1) * slot_cap + slot_of
        placing = jnp.any(
            slot_range[:, None, None] == target.reshape(row_count, choose_count)[None], -1
        ).astype(jnp.bfloat16)
        outbound = jnp.dot(placing, mlp_in, preferred_element_type=jnp.float32).astype(jnp.bfloat16)
        outbound = outbound.reshape(expert_count, slot_cap, model_width)
        batch = lax.all_to_all(outbound, "replica", split_axis=0, concat_axis=0, tiled=True)
        source_count = batch.shape[0]
        slot_count = batch.shape[1]
        flat_in = batch.reshape(source_count * slot_count, batch.shape[2])
        gate_part = jnp.dot(flat_in, gate_up[0], preferred_element_type=jnp.float32)
        up_part = jnp.dot(flat_in, gate_up[1], preferred_element_type=jnp.float32)
        hidden = (jax.nn.silu(gate_part) * up_part).astype(jnp.bfloat16)
        partial_out = jnp.dot(hidden, down_weight, preferred_element_type=jnp.float32).reshape(
            source_count, slot_count, model_width
        )
        summed = lax.psum(partial_out.astype(jnp.bfloat16), "expert")
        returned = lax.all_to_all(summed, "replica", split_axis=0, concat_axis=0, tiled=True)
        picked = returned.reshape(expert_count * slot_cap, model_width)[target]
        picked = picked.reshape(row_count, choose_count, model_width).astype(jnp.float32)
        finished = (after_attn.astype(jnp.float32) + jnp.sum(weight[..., None] * picked, 1)).astype(
            jnp.bfloat16
        )
        share_out = lax.dynamic_slice_in_dim(finished, lane_index * share_width, share_width, 1)
        outgoing = finished
        outgoing, share_out, new_entry = (outgoing, share_out, new_entry)
        fresh = jnp.where(active, fresh.at[step_at].set(new_entry), fresh)
        results = jnp.where(active, results.at[step_at].set(share_out), results)
        if tick_index + 1 < tick_total:
            incoming = shifted_2(outgoing, "section", 1)
    return (results[None], fresh[None])


def solution(mesh):
    return jax.shard_map(
        local,
        mesh=mesh,
        in_specs=(
            P(None, "replica", None),
            P("section", None),
            P("section", None, "expert"),
            P("section", None, "expert", None),
            P("section", "expert"),
            P("section", "expert", None),
            P("section", None),
            P("section", None, None),
            P("section", "replica", None, None, "expert"),
            P("section", "replica", "expert", None),
            P("section", "replica", None, "expert", None),
            P("replica", None),
            P("replica"),
            P("section", None, "replica", None),
        ),
        out_specs=(
            P("section", None, "replica", "expert"),
            P("section", None, "replica", "expert", None),
        ),
        check_vma=False,
    )
```

profile of v0, /device:TPU:1, one launch (start us, length us, event | category | flops | bytes accessed | tf_op | source)
XLA Modules:
  0.0 1151.9 jit_solution(12323026308020968581)
XLA Ops:
  8.1 9.5 collective-permute-start
  29.7 1.9 collective-permute-start.1
  32.5 7.0 collective-permute-done.1
  43.5 38.7 %psum.84 = bf16[16,1536]{1,0:T(8,128)(2,1)S(1)} all-reduce(bf16[16,1536]{1,0:T(8,128)(2,1)S(1)} %convolution_convert_fusion.17), channel_id=1, replica_groups=mesh['section'=4,'replica'=16,'expert'=8] {'expert'}, use_global_device_ids=true, to_apply=%region_7.8 | all-reduce | flops 24576 | bytes 98304 | tf_op jit(solution)/shard_map/psum | solution.py:157
  83.4 3.6 all-to-all-start
  87.8 9.2 all-to-all-done
  102.7 97.5 %all-reduce.7.cloned.1.call-done = bf16[16,5,1536]{2,0,1:T(8,128)(2,1)} async-done(((bf16[16,5,1536]{2,0,1:T(8,128)(2,1)}), bf16[16,5,1536]{2,0,1:T(8,128)(2,1)}) %all-reduce.7.cloned.1.call-update) | async-done | bytes 245776 | tf_op jit(solution)/shard_map/psum | solution.py:187
  200.2 1.8 copy.261
  202.1 6.5 all-to-all-start.1
  211.7 9.4 all-to-all-done.1
  225.7 3.7 collective-permute-start.2
  236.0 35.0 %psum.86 = bf16[16,1536]{1,0:T(8,128)(2,1)S(1)} all-reduce(bf16[16,1536]{1,0:T(8,128)(2,1)S(1)} %convolution_convert_fusion.16), channel_id=1, replica_groups=mesh['section'=4,'replica'=16,'expert'=8] {'expert'}, use_global_device_ids=true, to_apply=%region_23.24 | all-reduce | flops 24576 | bytes 98304 | tf_op jit(solution)/shard_map/psum | solution.py:157
  273.0 3.9 all-to-all-start.2
  277.7 11.1 all-to-all-done.2
  294.4 93.6 %all-reduce.9.cloned.1.call-done = bf16[16,5,1536]{2,0,1:T(8,128)(2,1)} async-done(((bf16[16,5,1536]{2,0,1:T(8,128)(2,1)}), bf16[16,5,1536]{2,0,1:T(8,128)(2,1)}) %all-reduce.9.cloned.1.call-update) | async-done | bytes 245776 | tf_op jit(solution)/shard_map/psum | solution.py:187
  388.0 1.8 copy.272
  389.8 6.5 all-to-all-start.3
  399.5 9.4 all-to-all-done.3
  413.5 3.3 collective-permute-start.3
  421.9 35.0 %psum.88 = bf16[16,1536]{1,0:T(8,128)(2,1)S(1)} all-reduce(bf16[16,1536]{1,0:T(8,128)(2,1)S(1)} %convolution_convert_fusion.15), channel_id=1, replica_groups=mesh['section'=4,'replica'=16,'expert'=8] {'expert'}, use_global_device_ids=true, to_apply=%region_39.40 | all-reduce | flops 24576 | bytes 98304 | tf_op jit(solution)/shard_map/psum | solution.py:157
  458.2 3.9 all-to-all-start.4
  462.7 11.3 all-to-all-done.4
  479.2 93.0 %all-reduce.11.cloned.1.call-done = bf16[16,5,1536]{2,0,1:T(8,128)(2,1)} async-done(((bf16[16,5,1536]{2,0,1:T(8,128)(2,1)}), bf16[16,5,1536]{2,0,1:T(8,128)(2,1)}) %all-reduce.11.cloned.1.call-update) | async-done | bytes 245776 | tf_op jit(solution)/shard_map/psum | solution.py:187
  572.2 1.8 copy.283
  574.1 6.5 all-to-all-start.5
  584.3 8.8 all-to-all-done.5
  597.7 3.1 collective-permute-start.4
  606.1 35.0 %psum.90 = bf16[16,1536]{1,0:T(8,128)(2,1)S(1)} all-reduce(bf16[16,1536]{1,0:T(8,128)(2,1)S(1)} %convolution_convert_fusion.14), channel_id=1, replica_groups=mesh['section'=4,'replica'=16,'expert'=8] {'expert'}, use_global_device_ids=true, to_apply=%region_55.56 | all-reduce | flops 24576 | bytes 98304 | tf_op jit(solution)/shard_map/psum | solution.py:157
  642.4 3.9 all-to-all-start.6
  647.0 11.1 all-to-all-done.6
  663.8 92.7 %all-reduce.13.cloned.1.call-done = bf16[16,5,1536]{2,0,1:T(8,128)(2,1)} async-done(((bf16[16,5,1536]{2,0,1:T(8,128)(2,1)}), bf16[16,5,1536]{2,0,1:T(8,128)(2,1)}) %all-reduce.13.cloned.1.call-update) | async-done | bytes 245776 | tf_op jit(solution)/shard_map/psum | solution.py:187
  756.5 1.8 copy.294
  758.3 6.5 all-to-all-start.7
  768.0 9.4 all-to-all-done.7
  782.0 3.1 collective-permute-start.5
  790.4 35.0 %psum.92 = bf16[16,1536]{1,0:T(8,128)(2,1)S(1)} all-reduce(bf16[16,1536]{1,0:T(8,128)(2,1)S(1)} %convolution_convert_fusion.13), channel_id=1, replica_groups=mesh['section'=4,'replica'=16,'expert'=8] {'expert'}, use_global_device_ids=true, to_apply=%region_71.72 | all-reduce | flops 24576 | bytes 98304 | tf_op jit(solution)/shard_map/psum | solution.py:157
  826.7 3.9 all-to-all-start.8
  831.4 11.0 all-to-all-done.8
  848.2 92.5 %all-reduce.15.cloned.1.call-done = bf16[16,5,1536]{2,0,1:T(8,128)(2,1)} async-done(((bf16[16,5,1536]{2,0,1:T(8,128)(2,1)}), bf16[16,5,1536]{2,0,1:T(8,128)(2,1)}) %all-reduce.15.cloned.1.call-update) | async-done | bytes 245776 | tf_op jit(solution)/shard_map/psum | solution.py:187
  942.5 6.5 all-to-all-start.9
  953.5 8.1 all-to-all-done.9
  966.2 3.1 collective-permute-start.6
  974.5 35.1 %psum.94 = bf16[16,1536]{1,0:T(8,128)(2,1)S(1)} all-reduce(bf16[16,1536]{1,0:T(8,128)(2,1)S(1)} %convolution_convert_fusion.12), channel_id=1, replica_groups=mesh['section'=4,'replica'=16,'expert'=8] {'expert'}, use_global_device_ids=true, to_apply=%region_87.88 | all-reduce | flops 24576 | bytes 98304 | tf_op jit(solution)/shard_map/psum | solution.py:157
  1010.8 3.9 all-to-all-start.10
  1020.6 6.0 all-to-all-done.10
  1030.4 91.2 %all-reduce.17.cloned.1.call-done = bf16[16,5,1536]{2,0,1:T(8,128)(2,1)} async-done(((bf16[16,5,1536]{2,0,1:T(8,128)(2,1)}), bf16[16,5,1536]{2,0,1:T(8,128)(2,1)}) %all-reduce.17.cloned.1.call-update) | async-done | bytes 245776 | tf_op jit(solution)/shard_map/psum | solution.py:187
  1123.4 6.5 all-to-all-start.11
  1131.1 11.3 all-to-all-done.11
  (609 shorter events, 141.6 us)
Async XLA Ops:
  7.2 93.7 %copy-start = (bf16[1,1,256,1536]{3,2,1,0:T(8,128)(2,1)S(1)}, bf16[1,1,256,1536]{3,2,1,0:T(8,128)(2,1)}, u32[]{:S(2)}) copy-start(bf16[1,1,256,1536]{3,2,1,0:T(8,128)(2,1)} %param.59) | copy-start | bytes 2359300
  8.1 20.6 %collective-permute-start = (s32[4,8]{0,1:T(8,128)S(1)}, s32[4,8]{0,1:T(8,128)S(1)}, u32[]{:S(2)}, u32[]{:S(2)}) collective-permute-start(s32[4,8]{0,1:T(8,128)S(1)} %slice.535), channel_id=1, source_target_pairs={{0,120},{8,0},{16,8},{24,16},{32,24},{40,32},{48,40},{56,48},{64,5... | collective-permute-start | bytes 392 | tf_op jit(solution)/shard_map/ppermute | solution.py:14
  21.1 66.6 %copy-start.52 = (s32[1,1,16,4]{2,3,1,0:T(4,128)}, s32[1,1,16,4]{2,3,1,0:T(4,128)S(1)}, u32[]{:S(2)}) copy-start(s32[1,1,16,4]{2,3,1,0:T(4,128)S(1)} %get-tuple-element.289) | copy-start | bytes 772
  26.7 182.5 %copy-start.16 = (bf16[3,16,1,128]{3,1,2,0:T(8,128)(2,1)}, bf16[3,16,1,128]{3,1,2,0:T(8,128)(2,1)S(1)}, u32[]{:S(2)}) copy-start(bf16[3,16,1,128]{3,1,2,0:T(8,128)(2,1)S(1)} %constant_dynamic-update-slice_fusion.11) | copy-start | bytes 36868
  29.7 9.7 collective-permute-start.1
  82.3 127.5 %copy-start.15 = (bf16[16,1536]{1,0:T(8,128)(2,1)}, bf16[16,1536]{1,0:T(8,128)(2,1)S(1)}, u32[]{:S(2)}) copy-start(bf16[16,1536]{1,0:T(8,128)(2,1)S(1)} %get-tuple-element.245) | copy-start | bytes 147460
  83.4 13.5 %all-to-all-start = ((bf16[16,5,1536]{2,1,0:T(8,128)(2,1)}), bf16[16,5,1536]{2,1,0:T(8,128)(2,1)S(1)}, u32[]{:S(2)}, u32[]{:S(2)}) async-start(bf16[16,5,1536]{2,1,0:T(8,128)(2,1)} %reshape.2989), calls=%async_computation | async-start | bytes 786432 | tf_op jit(solution)/shard_map/all_to_all | solution.py:177
  87.0 113.2 %all-reduce.7.cloned.1.call-start = ((), (), s32[]{:S(2)}) async-start(), calls=%async_computation.12 | async-start | bytes 491520 | tf_op jit(solution)/shard_map/psum | solution.py:187
  202.1 19.0 %all-to-all-start.1 = ((bf16[16,5,1536]{2,1,0:T(8,128)(2,1)}), bf16[16,5,1536]{2,1,0:T(8,128)(2,1)S(1)}, u32[]{:S(2)}, u32[]{:S(2)}) async-start(bf16[16,5,1536]{2,1,0:T(8,128)(2,1)} %copy.261), calls=%async_computation.1 | async-start | bytes 786432 | tf_op jit(solution)/shard_map/all_to_all | solution.py:188
  225.7 4.6 collective-permute-start.2
  235.5 41.6 %copy-start.50 = (s32[1,1,16,4]{2,3,1,0:T(4,128)S(1)}, s32[1,1,16,4]{2,3,1,0:T(4,128)}, u32[]{:S(2)}) copy-start(s32[1,1,16,4]{2,3,1,0:T(4,128)} %get-tuple-element.287) | copy-start | bytes 772
  235.7 41.9 %copy-start.86 = (s32[64]{0:T(128)S(1)}, s32[64]{0:T(128)}, u32[]{:S(2)}) copy-start(s32[64]{0:T(128)} %copy-done.85) | copy-start | bytes 772
  271.1 127.2 %copy-start.13 = (bf16[16,1536]{1,0:T(8,128)(2,1)}, bf16[16,1536]{1,0:T(8,128)(2,1)S(1)}, u32[]{:S(2)}) copy-start(bf16[16,1536]{1,0:T(8,128)(2,1)S(1)} %get-tuple-element.239) | copy-start | bytes 147460
  273.0 15.8 %all-to-all-start.2 = ((bf16[16,5,1536]{2,1,0:T(8,128)(2,1)}), bf16[16,5,1536]{2,1,0:T(8,128)(2,1)S(1)}, u32[]{:S(2)}, u32[]{:S(2)}) async-start(bf16[16,5,1536]{2,1,0:T(8,128)(2,1)} %reshape.2996), calls=%async_computation.2 | async-start | bytes 786432 | tf_op jit(solution)/shard_map/all_to_all | solution.py:177
  276.8 111.1 %all-reduce.9.cloned.1.call-start = ((), (), s32[]{:S(2)}) async-start(), calls=%async_computation.13 | async-start | bytes 491520 | tf_op jit(solution)/shard_map/psum | solution.py:187
  292.6 104.3 %copy-start.83 = (s32[4]{0:T(128)S(1)}, s32[4]{0:T(128)}, u32[]{:S(2)}) copy-start(s32[4]{0:T(128)} %constant.446.clone.1) | copy-start | bytes 52
  292.6 105.8 %copy-start.104 = (bf16[1,1536,16]{1,2,0:T(8,128)(2,1)S(1)}, bf16[1,1536,16]{1,2,0:T(8,128)(2,1)}, u32[]{:S(2)}) copy-start(bf16[1,1536,16]{1,2,0:T(8,128)(2,1)} %param.57) | copy-start | bytes 147460
  292.6 105.9 %copy-start.53 = (s32[1,1,16,4]{2,3,1,0:T(4,128)S(1)}, s32[1,1,16,4]{2,3,1,0:T(4,128)}, u32[]{:S(2)}) copy-start(s32[1,1,16,4]{2,3,1,0:T(4,128)} %copy-done.52) | copy-start | bytes 772
  389.8 19.0 %all-to-all-start.3 = ((bf16[16,5,1536]{2,1,0:T(8,128)(2,1)}), bf16[16,5,1536]{2,1,0:T(8,128)(2,1)S(1)}, u32[]{:S(2)}, u32[]{:S(2)}) async-start(bf16[16,5,1536]{2,1,0:T(8,128)(2,1)} %copy.272), calls=%async_computation.3 | async-start | bytes 786432 | tf_op jit(solution)/shard_map/all_to_all | solution.py:188
  413.5 4.6 collective-permute-start.3
  457.0 125.3 %copy-start.14 = (bf16[16,1536]{1,0:T(8,128)(2,1)}, bf16[16,1536]{1,0:T(8,128)(2,1)S(1)}, u32[]{:S(2)}) copy-start(bf16[16,1536]{1,0:T(8,128)(2,1)S(1)} %get-tuple-element.233) | copy-start | bytes 147460
  458.2 15.8 %all-to-all-start.4 = ((bf16[16,5,1536]{2,1,0:T(8,128)(2,1)}), bf16[16,5,1536]{2,1,0:T(8,128)(2,1)S(1)}, u32[]{:S(2)}, u32[]{:S(2)}) async-start(bf16[16,5,1536]{2,1,0:T(8,128)(2,1)} %reshape.3004), calls=%async_computation.4 | async-start | bytes 786432 | tf_op jit(solution)/shard_map/all_to_all | solution.py:177
  462.1 110.1 %all-reduce.11.cloned.1.call-start = ((), (), s32[]{:S(2)}) async-start(), calls=%async_computation.14 | async-start | bytes 491520 | tf_op jit(solution)/shard_map/psum | solution.py:187
  477.8 105.5 %copy-start.51 = (s32[1,1,16,4]{2,3,1,0:T(4,128)S(1)}, s32[1,1,16,4]{2,3,1,0:T(4,128)}, u32[]{:S(2)}) copy-start(s32[1,1,16,4]{2,3,1,0:T(4,128)} %get-tuple-element.287) | copy-start | bytes 772
  479.0 105.2 %copy-start.93 = (s32[64]{0:T(128)}, s32[64]{0:T(128)S(1)}, u32[]{:S(2)}) copy-start(s32[64]{0:T(128)S(1)} %select_reduce_fusion.4) | copy-start | bytes 772
  574.1 19.0 %all-to-all-start.5 = ((bf16[16,5,1536]{2,1,0:T(8,128)(2,1)}), bf16[16,5,1536]{2,1,0:T(8,128)(2,1)S(1)}, u32[]{:S(2)}, u32[]{:S(2)}) async-start(bf16[16,5,1536]{2,1,0:T(8,128)(2,1)} %copy.283), calls=%async_computation.5 | async-start | bytes 786432 | tf_op jit(solution)/shard_map/all_to_all | solution.py:188
  597.7 4.6 collective-permute-start.4
  641.2 125.7 %copy-start.12 = (bf16[16,1536]{1,0:T(8,128)(2,1)}, bf16[16,1536]{1,0:T(8,128)(2,1)S(1)}, u32[]{:S(2)}) copy-start(bf16[16,1536]{1,0:T(8,128)(2,1)S(1)} %get-tuple-element.227) | copy-start | bytes 147460
  642.4 15.8 %all-to-all-start.6 = ((bf16[16,5,1536]{2,1,0:T(8,128)(2,1)}), bf16[16,5,1536]{2,1,0:T(8,128)(2,1)S(1)}, u32[]{:S(2)}, u32[]{:S(2)}) async-start(bf16[16,5,1536]{2,1,0:T(8,128)(2,1)} %reshape.3012), calls=%async_computation.6 | async-start | bytes 786432 | tf_op jit(solution)/shard_map/all_to_all | solution.py:177
  646.2 110.2 %all-reduce.13.cloned.1.call-start = ((), (), s32[]{:S(2)}) async-start(), calls=%async_computation.15 | async-start | bytes 491520 | tf_op jit(solution)/shard_map/psum | solution.py:187
  662.0 103.5 %copy-start.84 = (s32[4]{0:T(128)S(1)}, s32[4]{0:T(128)}, u32[]{:S(2)}) copy-start(s32[4]{0:T(128)} %constant.446.clone.1) | copy-start | bytes 52
  662.0 104.9 %copy-start.105 = (bf16[1,1536,16]{1,2,0:T(8,128)(2,1)S(1)}, bf16[1,1536,16]{1,2,0:T(8,128)(2,1)}, u32[]{:S(2)}) copy-start(bf16[1,1536,16]{1,2,0:T(8,128)(2,1)} %param.57) | copy-start | bytes 147460
  662.0 105.0 %copy-start.49 = (s32[1,1,16,4]{2,3,1,0:T(4,128)S(1)}, s32[1,1,16,4]{2,3,1,0:T(4,128)}, u32[]{:S(2)}) copy-start(s32[1,1,16,4]{2,3,1,0:T(4,128)} %get-tuple-element.285) | copy-start | bytes 772
  758.3 19.0 %all-to-all-start.7 = ((bf16[16,5,1536]{2,1,0:T(8,128)(2,1)}), bf16[16,5,1536]{2,1,0:T(8,128)(2,1)S(1)}, u32[]{:S(2)}, u32[]{:S(2)}) async-start(bf16[16,5,1536]{2,1,0:T(8,128)(2,1)} %copy.294), calls=%async_computation.7 | async-start | bytes 786432 | tf_op jit(solution)/shard_map/all_to_all | solution.py:188
  782.0 4.6 collective-permute-start.5
  825.5 126.1 %copy-start.11 = (bf16[16,1536]{1,0:T(8,128)(2,1)}, bf16[16,1536]{1,0:T(8,128)(2,1)S(1)}, u32[]{:S(2)}) copy-start(bf16[16,1536]{1,0:T(8,128)(2,1)S(1)} %get-tuple-element.221) | copy-start | bytes 147460
  826.7 15.8 %all-to-all-start.8 = ((bf16[16,5,1536]{2,1,0:T(8,128)(2,1)}), bf16[16,5,1536]{2,1,0:T(8,128)(2,1)S(1)}, u32[]{:S(2)}, u32[]{:S(2)}) async-start(bf16[16,5,1536]{2,1,0:T(8,128)(2,1)} %reshape.3020), calls=%async_computation.8 | async-start | bytes 786432 | tf_op jit(solution)/shard_map/all_to_all | solution.py:177
  830.5 110.1 %all-reduce.15.cloned.1.call-start = ((), (), s32[]{:S(2)}) async-start(), calls=%async_computation.16 | async-start | bytes 491520 | tf_op jit(solution)/shard_map/psum | solution.py:187
  846.3 103.3 %copy-start.65 = (s32[1,1,16,4]{2,3,1,0:T(4,128)S(1)}, s32[1,1,16,4]{2,3,1,0:T(4,128)}, u32[]{:S(2)}) copy-start(s32[1,1,16,4]{2,3,1,0:T(4,128)} %get-tuple-element.214) | copy-start | bytes 772
  846.3 106.3 %copy-start.47 = (s32[1,1,16,4]{2,3,1,0:T(4,128)S(1)}, s32[1,1,16,4]{2,3,1,0:T(4,128)}, u32[]{:S(2)}) copy-start(s32[1,1,16,4]{2,3,1,0:T(4,128)} %get-tuple-element.293) | copy-start | bytes 772
  942.5 19.0 %all-to-all-start.9 = ((bf16[16,5,1536]{2,1,0:T(8,128)(2,1)}), bf16[16,5,1536]{2,1,0:T(8,128)(2,1)S(1)}, u32[]{:S(2)}, u32[]{:S(2)}) async-start(bf16[16,5,1536]{2,1,0:T(8,128)(2,1)} %copy.305), calls=%async_computation.9 | async-start | bytes 786432 | tf_op jit(solution)/shard_map/all_to_all | solution.py:188
  966.2 4.6 collective-permute-start.6
  974.5 52.3 %copy-start.103 = (bf16[1,1,2,1536,256]{4,3,2,1,0:T(8,128)(2,1)S(1)}, bf16[1,1,2,1536,256]{4,3,2,1,0:T(8,128)(2,1)}, u32[]{:S(2)}) copy-start(bf16[1,1,2,1536,256]{4,3,2,1,0:T(8,128)(2,1)} %param.58) | copy-start | bytes 4718596
  1010.8 15.8 %all-to-all-start.10 = ((bf16[16,5,1536]{2,1,0:T(8,128)(2,1)}), bf16[16,5,1536]{2,1,0:T(8,128)(2,1)S(1)}, u32[]{:S(2)}, u32[]{:S(2)}) async-start(bf16[16,5,1536]{2,1,0:T(8,128)(2,1)} %reshape.3028), calls=%async_computation.10 | async-start | bytes 786432 | tf_op jit(solution)/shard_map/all_to_all | solution.py:177
  1014.7 106.9 %all-reduce.17.cloned.1.call-start = ((), (), s32[]{:S(2)}) async-start(), calls=%async_computation.17 | async-start | bytes 491520 | tf_op jit(solution)/shard_map/psum | solution.py:187
  1027.2 102.7 %copy-start.106 = (bf16[1,1536,16]{1,2,0:T(8,128)(2,1)S(1)}, bf16[1,1536,16]{1,2,0:T(8,128)(2,1)}, u32[]{:S(2)}) copy-start(bf16[1,1536,16]{1,2,0:T(8,128)(2,1)} %param.57) | copy-start | bytes 147460
  1027.3 102.9 %copy-start.45 = (s32[1,1,16,4]{2,3,1,0:T(4,128)S(1)}, s32[1,1,16,4]{2,3,1,0:T(4,128)}, u32[]{:S(2)}) copy-start(s32[1,1,16,4]{2,3,1,0:T(4,128)} %get-tuple-element.215) | copy-start | bytes 772
  1123.4 19.0 %all-to-all-start.11 = ((bf16[16,5,1536]{2,1,0:T(8,128)(2,1)}), bf16[16,5,1536]{2,1,0:T(8,128)(2,1)S(1)}, u32[]{:S(2)}, u32[]{:S(2)}) async-start(bf16[16,5,1536]{2,1,0:T(8,128)(2,1)} %copy.316), calls=%async_computation.11 | async-start | bytes 786432 | tf_op jit(solution)/shard_map/all_to_all | solution.py:188
  (89 other events, 1390.9 us)
Sparse Core Ops, SparseCore 0:
  102.0 98.1 all-reduce.6
  293.8 94.1 all-reduce.8
  479.0 93.1 all-reduce.10
  663.2 93.2 all-reduce.12
  847.4 93.1 all-reduce.14
  1028.4 93.1 all-reduce.16
where the time goes:
time: 1160 us; the launch traced here: 1150 us
  waiting for transfers between devices  686 us (59%)
  blocking collectives  214 us (18%)
  starting transfers between devices  90.3 us (8%)
  other arithmetic  52.8 us (5%)
  local copies, waits for them, and re-layouts  50.7 us (4%)
  matrix products  41.9 us (4%)
  between operations  16.2 us (1%)
    psum x6, waiting for transfers between devices, local(): summed = lax.psum(partial_out.astype(jnp.bfloat16), 'expert')  560 us
    psum x6, blocking collectives, local(): lax.psum(jnp.dot(attended, out_weight, preferred_element_type=jnp.float32...  214 us
    all_to_all x6, waiting for transfers between devices, local(): lax.all_to_all(outbound, 'replica', split_axis=0, concat_axis=0, tiled=True)  59.6 us
    all_to_all x6, waiting for transfers between devices, local(): lax.all_to_all(summed, 'replica', split_axis=0, concat_axis=0, tiled=True)  56.2 us
    all_to_all x6, starting transfers between devices, local(): lax.all_to_all(summed, 'replica', split_axis=0, concat_axis=0, tiled=True)  39.2 us
  transfers between devices with their start and end apart: 25, of which 24 were waited for; matrix products, arithmetic and copies ran while one was open for 4% of the time, Pallas kernels for 0%

commit v1 on v0

--- a/solution.py
+++ b/solution.py
@@ -7,6 +7,7 @@
 EPS = 1e-05
 THETA = 150000.0
 NEG = -1e30
+end_the_strings = lambda mine: lax.all_gather(mine, axis_name="expert").sum(axis=0)
 
 
 def shifted(shard, axis, by):
@@ -184,7 +185,7 @@
         partial_out = jnp.dot(hidden, down_weight, preferred_element_type=jnp.float32).reshape(
             source_count, slot_count, model_width
         )
-        summed = lax.psum(partial_out.astype(jnp.bfloat16), "expert")
+        summed = end_the_strings(partial_out.astype(jnp.bfloat16))
         returned = lax.all_to_all(summed, "replica", split_axis=0, concat_axis=0, tiled=True)
         picked = returned.reshape(expert_count * slot_cap, model_width)[target]
         picked = picked.reshape(row_count, choose_count, model_width).astype(jnp.float32)

time: 1160 us -> 921 us (0.79)
  waiting for transfers between devices: 686 us -> 419 us
  blocking collectives: 214 us -> 304 us
  starting transfers between devices: 90.3 us -> 56.6 us
  local copies, waits for them, and re-layouts: 50.7 us -> 28.2 us
    psum x6 -> x0, waiting for transfers between devices: 560 us -> none  [local(): summed = lax.psum(partial_out.astype(jnp.bfloat16), 'expert')]
    all_gather x0 -> x6, waiting for transfers between devices: none -> 349 us  [lax.all_gather(mine, axis_name='expert').sum(axis=0)]
    all_to_all x0 -> x6, blocking collectives: none -> 80.4 us  [local(): lax.all_to_all(outbound, 'replica', split_axis=0, concat_axis=0, tiled=True)]
    all_to_all x6 -> x0, waiting for transfers between devices: 59.6 us -> none  [local(): lax.all_to_all(outbound, 'replica', split_axis=0, concat_axis=0, tiled=True)]
    all_to_all x6 -> x0, starting transfers between devices: 22.9 us -> none  [local(): lax.all_to_all(outbound, 'replica', split_axis=0, concat_axis=0, tiled=True)]
  transfers between devices with their start and end apart: 25 -> 19, of which waited for: 24 -> 18; matrix products, arithmetic and copies ran while one was open for 4% -> 4% of each run, Pallas kernels for 0% -> 0%
where the time goes in v1:
time: 921 us; the launch traced here: 918 us
  waiting for transfers between devices  419 us (45%)
  blocking collectives  304 us (33%)
  starting transfers between devices  56.6 us (6%)
  other arithmetic  54.1 us (6%)
  matrix products  39.5 us (4%)
  local copies, waits for them, and re-layouts  28.2 us (3%)
  between operations  16.8 us (2%)
    all_gather x6, waiting for transfers between devices, lax.all_gather(mine, axis_name='expert').sum(axis=0)  349 us
    psum x6, blocking collectives, local(): lax.psum(jnp.dot(attended, out_weight, preferred_element_type=jnp.float32...  223 us
    all_to_all x6, blocking collectives, local(): lax.all_to_all(outbound, 'replica', split_axis=0, concat_axis=0, tiled=True)  80.4 us
    all_to_all x6, waiting for transfers between devices, local(): lax.all_to_all(summed, 'replica', split_axis=0, concat_axis=0, tiled=True)  58.2 us
    all_to_all x6, starting transfers between devices, local(): lax.all_to_all(summed, 'replica', split_axis=0, concat_axis=0, tiled=True)  29.1 us
  transfers between devices with their start and end apart: 19, of which 18 were waited for; matrix products, arithmetic and copies ran while one was open for 4% of the time, Pallas kernels for 0%

profile of v1, /device:TPU:1, one launch (start us, length us, event | category | flops | bytes accessed | tf_op | source)
XLA Modules:
  0.0 918.1 jit_solution(3386102499760962637)
XLA Ops:
  8.1 9.5 %collective-permute-start = (s32[4,8]{0,1:T(8,128)S(1)}, s32[4,8]{0,1:T(8,128)S(1)}, u32[]{:S(2)}, u32[]{:S(2)}) collective-permute-start(s32[4,8]{0,1:T(8,128)S(1)} %slice.535), channel_id=1, source_target_pairs={{0,120},{8,0},{16,8},{24,16},{32,24},{40,32},{48,40},{56,48},{64,5... | collective-permute-start | bytes 392 | tf_op jit(solution)/shard_map/ppermute | solution.py:15
  19.7 1.5 broadcast_multiply_fusion
  22.7 1.5 copy.319
  29.5 1.9 collective-permute-start.1
  32.2 7.0 collective-permute-done.1
  42.4 38.7 %psum.42 = bf16[16,1536]{1,0:T(8,128)(2,1)S(1)} all-reduce(bf16[16,1536]{1,0:T(8,128)(2,1)S(1)} %convolution_convert_fusion.17), channel_id=1, replica_groups=mesh['section'=4,'replica'=16,'expert'=8] {'expert'}, use_global_device_ids=true, to_apply=%region_7.8 | all-reduce | flops 24576 | bytes 98304 | tf_op jit(solution)/shard_map/psum | solution.py:158
  82.0 12.6 %all_to_all.60 = bf16[16,5,1536]{2,1,0:T(8,128)(2,1)S(1)} all-to-all(bf16[16,5,1536]{2,1,0:T(8,128)(2,1)S(1)} %reshape.2989), channel_id=1, replica_groups=mesh['section'=4,'replica'=16,'expert'=8] {'replica'}, dimensions={0} | all-to-all | bytes 491520 | tf_op jit(solution)/shard_map/all_to_all | solution.py:178
  100.1 61.3 %all-gather.13.cloned.1.call-done = bf16[128,5,1536]{2,0,1:T(8,128)(2,1)} async-done(((bf16[16,5,1536]{2,0,1:T(8,128)(2,1)}), bf16[128,5,1536]{2,0,1:T(8,128)(2,1)}) %all-gather.13.cloned.1.call-update) | async-done | bytes 1966096 | tf_op jit(solution)/shard_map/all_gather | solution.py:10
  161.5 1.9 reduce_sum.536
  164.3 4.8 all-to-all-start.1
  170.9 10.2 %all-to-all-done.1 = bf16[16,5,1536]{2,1,0:T(8,128)(2,1)S(1)} async-done(((bf16[16,5,1536]{2,1,0:T(8,128)(2,1)}), bf16[16,5,1536]{2,1,0:T(8,128)(2,1)S(1)}, u32[]{:S(2)}, u32[]{:S(2)}) %all-to-all-start.1) | async-done | bytes 245792 | tf_op jit(solution)/shard_map/all_to_all | solution.py:189
  182.5 3.2 collective-permute-start.2
  193.5 36.9 %psum.43 = bf16[16,1536]{1,0:T(8,128)(2,1)S(1)} all-reduce(bf16[16,1536]{1,0:T(8,128)(2,1)S(1)} %convolution_convert_fusion.16), channel_id=1, replica_groups=mesh['section'=4,'replica'=16,'expert'=8] {'expert'}, use_global_device_ids=true, to_apply=%region_23.24 | all-reduce | flops 24576 | bytes 98304 | tf_op jit(solution)/shard_map/psum | solution.py:158
  231.2 13.5 %all_to_all.61 = bf16[16,5,1536]{2,1,0:T(8,128)(2,1)S(1)} all-to-all(bf16[16,5,1536]{2,1,0:T(8,128)(2,1)S(1)} %reshape.2996), channel_id=1, replica_groups=mesh['section'=4,'replica'=16,'expert'=8] {'replica'}, dimensions={0} | all-to-all | bytes 491520 | tf_op jit(solution)/shard_map/all_to_all | solution.py:178
  249.7 58.9 %all-gather.15.cloned.1.call-done = bf16[128,5,1536]{2,0,1:T(8,128)(2,1)} async-done(((bf16[16,5,1536]{2,0,1:T(8,128)(2,1)}), bf16[128,5,1536]{2,0,1:T(8,128)(2,1)}) %all-gather.15.cloned.1.call-update) | async-done | bytes 1966096 | tf_op jit(solution)/shard_map/all_gather | solution.py:10
  308.6 1.9 reduce_sum.547
  311.4 4.8 all-to-all-start.3
  319.4 8.9 all-to-all-done.3
  329.7 3.3 collective-permute-start.3
  338.7 36.9 %psum.44 = bf16[16,1536]{1,0:T(8,128)(2,1)S(1)} all-reduce(bf16[16,1536]{1,0:T(8,128)(2,1)S(1)} %convolution_convert_fusion.15), channel_id=1, replica_groups=mesh['section'=4,'replica'=16,'expert'=8] {'expert'}, use_global_device_ids=true, to_apply=%region_39.40 | all-reduce | flops 24576 | bytes 98304 | tf_op jit(solution)/shard_map/psum | solution.py:158
  376.4 13.6 %all_to_all.62 = bf16[16,5,1536]{2,1,0:T(8,128)(2,1)S(1)} all-to-all(bf16[16,5,1536]{2,1,0:T(8,128)(2,1)S(1)} %reshape.3004), channel_id=1, replica_groups=mesh['section'=4,'replica'=16,'expert'=8] {'replica'}, dimensions={0} | all-to-all | bytes 491520 | tf_op jit(solution)/shard_map/all_to_all | solution.py:178
  394.9 58.9 %all-gather.17.cloned.1.call-done = bf16[128,5,1536]{2,0,1:T(8,128)(2,1)} async-done(((bf16[16,5,1536]{2,0,1:T(8,128)(2,1)}), bf16[128,5,1536]{2,0,1:T(8,128)(2,1)}) %all-gather.17.cloned.1.call-update) | async-done | bytes 1966096 | tf_op jit(solution)/shard_map/all_gather | solution.py:10
  453.8 1.9 reduce_sum.558
  456.6 4.8 all-to-all-start.5
  463.8 9.6 %all-to-all-done.5 = bf16[16,5,1536]{2,1,0:T(8,128)(2,1)S(1)} async-done(((bf16[16,5,1536]{2,1,0:T(8,128)(2,1)}), bf16[16,5,1536]{2,1,0:T(8,128)(2,1)S(1)}, u32[]{:S(2)}, u32[]{:S(2)}) %all-to-all-start.5) | async-done | bytes 245792 | tf_op jit(solution)/shard_map/all_to_all | solution.py:189
  474.9 3.1 collective-permute-start.4
  483.7 36.9 %psum.45 = bf16[16,1536]{1,0:T(8,128)(2,1)S(1)} all-reduce(bf16[16,1536]{1,0:T(8,128)(2,1)S(1)} %convolution_convert_fusion.14), channel_id=1, replica_groups=mesh['section'=4,'replica'=16,'expert'=8] {'expert'}, use_global_device_ids=true, to_apply=%region_55.56 | all-reduce | flops 24576 | bytes 98304 | tf_op jit(solution)/shard_map/psum | solution.py:158
  521.7 13.6 %all_to_all.63 = bf16[16,5,1536]{2,1,0:T(8,128)(2,1)S(1)} all-to-all(bf16[16,5,1536]{2,1,0:T(8,128)(2,1)S(1)} %reshape.3012), channel_id=1, replica_groups=mesh['section'=4,'replica'=16,'expert'=8] {'replica'}, dimensions={0} | all-to-all | bytes 491520 | tf_op jit(solution)/shard_map/all_to_all | solution.py:178
  540.2 58.9 %all-gather.19.cloned.1.call-done = bf16[128,5,1536]{2,0,1:T(8,128)(2,1)} async-done(((bf16[16,5,1536]{2,0,1:T(8,128)(2,1)}), bf16[128,5,1536]{2,0,1:T(8,128)(2,1)}) %all-gather.19.cloned.1.call-update) | async-done | bytes 1966096 | tf_op jit(solution)/shard_map/all_gather | solution.py:10
  599.1 1.9 reduce_sum.569
  601.9 4.8 all-to-all-start.7
  609.9 8.9 all-to-all-done.7
  620.2 3.1 collective-permute-start.5
  629.1 36.9 %psum.46 = bf16[16,1536]{1,0:T(8,128)(2,1)S(1)} all-reduce(bf16[16,1536]{1,0:T(8,128)(2,1)S(1)} %convolution_convert_fusion.13), channel_id=1, replica_groups=mesh['section'=4,'replica'=16,'expert'=8] {'expert'}, use_global_device_ids=true, to_apply=%region_71.72 | all-reduce | flops 24576 | bytes 98304 | tf_op jit(solution)/shard_map/psum | solution.py:158
  666.9 13.5 %all_to_all.64 = bf16[16,5,1536]{2,1,0:T(8,128)(2,1)S(1)} all-to-all(bf16[16,5,1536]{2,1,0:T(8,128)(2,1)S(1)} %reshape.3020), channel_id=1, replica_groups=mesh['section'=4,'replica'=16,'expert'=8] {'replica'}, dimensions={0} | all-to-all | bytes 491520 | tf_op jit(solution)/shard_map/all_to_all | solution.py:178
  685.3 58.9 %all-gather.21.cloned.1.call-done = bf16[128,5,1536]{2,0,1:T(8,128)(2,1)} async-done(((bf16[16,5,1536]{2,0,1:T(8,128)(2,1)}), bf16[128,5,1536]{2,0,1:T(8,128)(2,1)}) %all-gather.21.cloned.1.call-update) | async-done | bytes 1966096 | tf_op jit(solution)/shard_map/all_gather | solution.py:10
  744.2 1.9 reduce_sum.580
  747.0 4.8 all-to-all-start.9
  754.3 9.6 %all-to-all-done.9 = bf16[16,5,1536]{2,1,0:T(8,128)(2,1)S(1)} async-done(((bf16[16,5,1536]{2,1,0:T(8,128)(2,1)}), bf16[16,5,1536]{2,1,0:T(8,128)(2,1)S(1)}, u32[]{:S(2)}, u32[]{:S(2)}) %all-to-all-start.9) | async-done | bytes 245792 | tf_op jit(solution)/shard_map/all_to_all | solution.py:189
  765.3 3.1 collective-permute-start.6
  774.3 36.9 %psum.47 = bf16[16,1536]{1,0:T(8,128)(2,1)S(1)} all-reduce(bf16[16,1536]{1,0:T(8,128)(2,1)S(1)} %convolution_convert_fusion.12), channel_id=1, replica_groups=mesh['section'=4,'replica'=16,'expert'=8] {'expert'}, use_global_device_ids=true, to_apply=%region_87.88 | all-reduce | flops 24576 | bytes 98304 | tf_op jit(solution)/shard_map/psum | solution.py:158
  811.7 13.5 %all_to_all.65 = bf16[16,5,1536]{2,1,0:T(8,128)(2,1)S(1)} all-to-all(bf16[16,5,1536]{2,1,0:T(8,128)(2,1)S(1)} %reshape.3028), channel_id=1, replica_groups=mesh['section'=4,'replica'=16,'expert'=8] {'replica'}, dimensions={0} | all-to-all | bytes 491520 | tf_op jit(solution)/shard_map/all_to_all | solution.py:178
  832.3 1.4 select_select_fusion.4
  835.1 1.4 select_select_fusion.2
  837.3 51.7 %all-gather.23.cloned.1.call-done = bf16[128,5,1536]{2,0,1:T(8,128)(2,1)} async-done(((bf16[16,5,1536]{2,0,1:T(8,128)(2,1)}), bf16[128,5,1536]{2,0,1:T(8,128)(2,1)}) %all-gather.23.cloned.1.call-update) | async-done | bytes 1966096 | tf_op jit(solution)/shard_map/all_gather | solution.py:10
  889.0 1.9 reduce_sum.591
  891.8 4.8 all-to-all-start.11
  897.8 10.9 %all-to-all-done.11 = bf16[16,5,1536]{2,1,0:T(8,128)(2,1)S(1)} async-done(((bf16[16,5,1536]{2,1,0:T(8,128)(2,1)}), bf16[16,5,1536]{2,1,0:T(8,128)(2,1)S(1)}, u32[]{:S(2)}, u32[]{:S(2)}) %all-to-all-start.11) | async-done | bytes 245792 | tf_op jit(solution)/shard_map/all_to_all | solution.py:189
  (671 shorter events, 110.4 us)
Async XLA Ops:
  7.2 90.4 %copy-start = (bf16[1,1,256,1536]{3,2,1,0:T(8,128)(2,1)S(1)}, bf16[1,1,256,1536]{3,2,1,0:T(8,128)(2,1)}, u32[]{:S(2)}) copy-start(bf16[1,1,256,1536]{3,2,1,0:T(8,128)(2,1)} %param.59) | copy-start | bytes 2359300
  7.2 17.0 %copy-start.3 = (bf16[3,16,1536]{2,1,0:T(8,128)(2,1)S(1)}, bf16[3,16,1536]{2,1,0:T(8,128)(2,1)}, u32[]{:S(2)}) copy-start(bf16[3,16,1536]{2,1,0:T(8,128)(2,1)} %param.50) | copy-start | bytes 442372
  7.2 17.2 %copy-start.92 = (f32[1,1536]{1,0:T(1,128)S(1)}, f32[1,1536]{1,0:T(1,128)}, u32[]{:S(2)}) copy-start(f32[1,1536]{1,0:T(1,128)} %param.51) | copy-start | bytes 18436
  7.2 17.6 %copy-start.2 = (bf16[1,1536,1,128]{3,1,2,0:T(8,128)(2,1)S(1)}, bf16[1,1536,1,128]{3,1,2,0:T(8,128)(2,1)}, u32[]{:S(2)}) copy-start(bf16[1,1536,1,128]{3,1,2,0:T(8,128)(2,1)} %param.53) | copy-start | bytes 1179652
  7.2 154.3 %all-gather.13.cloned.1.call-start = ((), (), s32[]{:S(2)}) async-start(), calls=%async_computation.12 | async-start | bytes 2211840 | tf_op jit(solution)/shard_map/all_gather | solution.py:10
  8.1 20.6 %collective-permute-start = (s32[4,8]{0,1:T(8,128)S(1)}, s32[4,8]{0,1:T(8,128)S(1)}, u32[]{:S(2)}, u32[]{:S(2)}) collective-permute-start(s32[4,8]{0,1:T(8,128)S(1)} %slice.535), channel_id=1, source_target_pairs={{0,120},{8,0},{16,8},{24,16},{32,24},{40,32},{48,40},{56,48},{64,5... | collective-permute-start | bytes 392 | tf_op jit(solution)/shard_map/ppermute | solution.py:15
  26.8 14.5 %copy-start.21 = (bf16[3,16,1,128]{3,1,2,0:T(8,128)(2,1)}, bf16[3,16,1,128]{3,1,2,0:T(8,128)(2,1)S(1)}, u32[]{:S(2)}) copy-start(bf16[3,16,1,128]{3,1,2,0:T(8,128)(2,1)S(1)} %constant_dynamic-update-slice_fusion.11) | copy-start | bytes 36868
  26.9 14.4 %copy-start.39 = (f32[1,4]{1,0:T(1,128)S(1)}, f32[1,4]{1,0:T(1,128)}, u32[]{:S(2)}) copy-start(f32[1,4]{1,0:T(1,128)} %param.54) | copy-start | bytes 52
  29.5 9.7 %collective-permute-start.1 = (bf16[32,16,1,128]{3,1,0,2:T(8,128)(2,1)S(1)}, bf16[32,16,1,128]{3,1,0,2:T(8,128)(2,1)}, u32[]{:S(2)}, u32[]{:S(2)}) collective-permute-start(bf16[32,16,1,128]{3,1,0,2:T(8,128)(2,1)S(1)} %bitcast.429), channel_id=1, source_target_pairs={{0,8},{8,16},{16,24},{24,32},{32,40},{40,48},{48,56},{56,64},{64,7... | collective-permute-start | bytes 393224 | tf_op jit(solution)/shard_map/ppermute | solution.py:15
  32.1 10.1 %copy-start.1 = (bf16[1,256,1536]{2,1,0:T(8,128)(2,1)S(1)}, bf16[1,256,1536]{2,1,0:T(8,128)(2,1)}, u32[]{:S(2)}) copy-start(bf16[1,256,1536]{2,1,0:T(8,128)(2,1)} %param.55) | copy-start | bytes 2359300
  99.3 62.2 %copy-start.114 = (s32[64]{0:T(128)}, s32[64]{0:T(128)S(1)}, u32[]{:S(2)}) copy-start(s32[64]{0:T(128)S(1)} %select_reduce_fusion.8) | copy-start | bytes 772
  164.3 16.9 %all-to-all-start.1 = ((bf16[16,5,1536]{2,1,0:T(8,128)(2,1)}), bf16[16,5,1536]{2,1,0:T(8,128)(2,1)S(1)}, u32[]{:S(2)}, u32[]{:S(2)}) async-start(bf16[16,5,1536]{2,1,0:T(8,128)(2,1)} %copy.333), calls=%async_computation.1 | async-start | bytes 786432 | tf_op jit(solution)/shard_map/all_to_all | solution.py:189
  169.1 139.4 %all-gather.15.cloned.1.call-start = ((), (), s32[]{:S(2)}) async-start(), calls=%async_computation.13 | async-start | bytes 2211840 | tf_op jit(solution)/shard_map/all_gather | solution.py:10
  182.2 10.2 %copy-start.40 = (f32[1,4]{1,0:T(1,128)S(1)}, f32[1,4]{1,0:T(1,128)}, u32[]{:S(2)}) copy-start(f32[1,4]{1,0:T(1,128)} %param.54) | copy-start | bytes 52
  182.5 4.4 collective-permute-start.2
  190.3 40.3 %copy-start.80 = (pred[80,16]{0,1:T(8,128)(4,1)S(1)}, pred[80,16]{0,1:T(8,128)(4,1)}, u32[]{:S(2)}) copy-start(pred[80,16]{0,1:T(8,128)(4,1)} %fusion.163) | copy-start | bytes 3844
  192.1 38.4 %copy-start.25 = (bf16[3,16,1,128]{3,1,2,0:T(8,128)(2,1)}, bf16[3,16,1,128]{3,1,2,0:T(8,128)(2,1)S(1)}, u32[]{:S(2)}) copy-start(bf16[3,16,1,128]{3,1,2,0:T(8,128)(2,1)S(1)} %constant_dynamic-update-slice_fusion.9) | copy-start | bytes 36868
  249.5 59.1 %copy-start.110 = (s32[64]{0:T(128)}, s32[64]{0:T(128)S(1)}, u32[]{:S(2)}) copy-start(s32[64]{0:T(128)S(1)} %select_reduce_fusion.6) | copy-start | bytes 772
  308.6 9.7 %copy-start.14 = (bf16[16,1536]{1,0:T(8,128)(2,1)S(1)}, bf16[16,1536]{1,0:T(8,128)(2,1)}, u32[]{:S(2)}) copy-start(bf16[16,1536]{1,0:T(8,128)(2,1)} %copy-done.13) | copy-start | bytes 147460
  308.6 9.7 %copy-start.126 = (f32[16]{0:T(128)S(1)}, f32[16]{0:T(128)}, u32[]{:S(2)}) copy-start(f32[16]{0:T(128)} %copy-done.125) | copy-start | bytes 196
  308.6 9.7 %copy-start.134 = (bf16[1,1536,16]{1,2,0:T(8,128)(2,1)S(1)}, bf16[1,1536,16]{1,2,0:T(8,128)(2,1)}, u32[]{:S(2)}) copy-start(bf16[1,1536,16]{1,2,0:T(8,128)(2,1)} %param.57) | copy-start | bytes 147460
  308.6 9.8 %copy-start.71 = (s32[1,1,16,4]{2,3,1,0:T(4,128)S(1)}, s32[1,1,16,4]{2,3,1,0:T(4,128)}, u32[]{:S(2)}) copy-start(s32[1,1,16,4]{2,3,1,0:T(4,128)} %get-tuple-element.291) | copy-start | bytes 772
  311.4 16.9 %all-to-all-start.3 = ((bf16[16,5,1536]{2,1,0:T(8,128)(2,1)}), bf16[16,5,1536]{2,1,0:T(8,128)(2,1)S(1)}, u32[]{:S(2)}, u32[]{:S(2)}) async-start(bf16[16,5,1536]{2,1,0:T(8,128)(2,1)} %copy.344), calls=%async_computation.3 | async-start | bytes 786432 | tf_op jit(solution)/shard_map/all_to_all | solution.py:189
  316.3 137.5 %all-gather.17.cloned.1.call-start = ((), (), s32[]{:S(2)}) async-start(), calls=%async_computation.14 | async-start | bytes 2211840 | tf_op jit(solution)/shard_map/all_gather | solution.py:10
  329.7 4.3 collective-permute-start.3
  336.0 39.7 %copy-start.83 = (pred[80,16]{0,1:T(8,128)(4,1)S(1)}, pred[80,16]{0,1:T(8,128)(4,1)}, u32[]{:S(2)}) copy-start(pred[80,16]{0,1:T(8,128)(4,1)} %fusion.164) | copy-start | bytes 3844
  337.3 38.5 %copy-start.29 = (bf16[3,16,1,128]{3,1,2,0:T(8,128)(2,1)}, bf16[3,16,1,128]{3,1,2,0:T(8,128)(2,1)S(1)}, u32[]{:S(2)}) copy-start(bf16[3,16,1,128]{3,1,2,0:T(8,128)(2,1)S(1)} %constant_dynamic-update-slice_fusion.7) | copy-start | bytes 36868
  394.7 61.9 %copy-start.112 = (s32[64]{0:T(128)}, s32[64]{0:T(128)S(1)}, u32[]{:S(2)}) copy-start(s32[64]{0:T(128)S(1)} %select_reduce_fusion.4) | copy-start | bytes 772
  456.6 16.9 %all-to-all-start.5 = ((bf16[16,5,1536]{2,1,0:T(8,128)(2,1)}), bf16[16,5,1536]{2,1,0:T(8,128)(2,1)S(1)}, u32[]{:S(2)}, u32[]{:S(2)}) async-start(bf16[16,5,1536]{2,1,0:T(8,128)(2,1)} %copy.355), calls=%async_computation.5 | async-start | bytes 786432 | tf_op jit(solution)/shard_map/all_to_all | solution.py:189
  461.4 137.7 %all-gather.19.cloned.1.call-start = ((), (), s32[]{:S(2)}) async-start(), calls=%async_computation.15 | async-start | bytes 2211840 | tf_op jit(solution)/shard_map/all_gather | solution.py:10
  474.9 4.3 collective-permute-start.4
  481.2 40.2 %copy-start.82 = (pred[80,16]{0,1:T(8,128)(4,1)S(1)}, pred[80,16]{0,1:T(8,128)(4,1)}, u32[]{:S(2)}) copy-start(pred[80,16]{0,1:T(8,128)(4,1)} %fusion.165) | copy-start | bytes 3844
  482.4 38.5 %copy-start.27 = (bf16[3,16,1,128]{3,1,2,0:T(8,128)(2,1)}, bf16[3,16,1,128]{3,1,2,0:T(8,128)(2,1)S(1)}, u32[]{:S(2)}) copy-start(bf16[3,16,1,128]{3,1,2,0:T(8,128)(2,1)S(1)} %constant_dynamic-update-slice_fusion.5) | copy-start | bytes 36868
  540.0 59.1 %copy-start.108 = (s32[64]{0:T(128)}, s32[64]{0:T(128)S(1)}, u32[]{:S(2)}) copy-start(s32[64]{0:T(128)S(1)} %select_reduce_fusion.2) | copy-start | bytes 772
  599.1 9.7 %copy-start.12 = (bf16[16,1536]{1,0:T(8,128)(2,1)S(1)}, bf16[16,1536]{1,0:T(8,128)(2,1)}, u32[]{:S(2)}) copy-start(bf16[16,1536]{1,0:T(8,128)(2,1)} %copy-done.11) | copy-start | bytes 147460
  599.1 9.7 %copy-start.124 = (f32[16]{0:T(128)S(1)}, f32[16]{0:T(128)}, u32[]{:S(2)}) copy-start(f32[16]{0:T(128)} %copy-done.123) | copy-start | bytes 196
  599.1 9.8 %copy-start.67 = (s32[1,1,16,4]{2,3,1,0:T(4,128)S(1)}, s32[1,1,16,4]{2,3,1,0:T(4,128)}, u32[]{:S(2)}) copy-start(s32[1,1,16,4]{2,3,1,0:T(4,128)} %get-tuple-element.287) | copy-start | bytes 772
  601.9 16.9 %all-to-all-start.7 = ((bf16[16,5,1536]{2,1,0:T(8,128)(2,1)}), bf16[16,5,1536]{2,1,0:T(8,128)(2,1)S(1)}, u32[]{:S(2)}, u32[]{:S(2)}) async-start(bf16[16,5,1536]{2,1,0:T(8,128)(2,1)} %copy.366), calls=%async_computation.7 | async-start | bytes 786432 | tf_op jit(solution)/shard_map/all_to_all | solution.py:189
  606.8 137.4 %all-gather.21.cloned.1.call-start = ((), (), s32[]{:S(2)}) async-start(), calls=%async_computation.16 | async-start | bytes 2211840 | tf_op jit(solution)/shard_map/all_gather | solution.py:10
  620.2 4.3 collective-permute-start.5
  626.5 39.7 %copy-start.84 = (pred[80,16]{0,1:T(8,128)(4,1)S(1)}, pred[80,16]{0,1:T(8,128)(4,1)}, u32[]{:S(2)}) copy-start(pred[80,16]{0,1:T(8,128)(4,1)} %fusion.166) | copy-start | bytes 3844
  627.7 38.5 %copy-start.31 = (bf16[3,16,1,128]{3,1,2,0:T(8,128)(2,1)}, bf16[3,16,1,128]{3,1,2,0:T(8,128)(2,1)S(1)}, u32[]{:S(2)}) copy-start(bf16[3,16,1,128]{3,1,2,0:T(8,128)(2,1)S(1)} %constant_dynamic-update-slice_fusion.3) | copy-start | bytes 36868
  685.1 59.1 %copy-start.106 = (s32[64]{0:T(128)}, s32[64]{0:T(128)S(1)}, u32[]{:S(2)}) copy-start(s32[64]{0:T(128)S(1)} %select_reduce_fusion) | copy-start | bytes 772
  747.0 16.9 %all-to-all-start.9 = ((bf16[16,5,1536]{2,1,0:T(8,128)(2,1)}), bf16[16,5,1536]{2,1,0:T(8,128)(2,1)S(1)}, u32[]{:S(2)}, u32[]{:S(2)}) async-start(bf16[16,5,1536]{2,1,0:T(8,128)(2,1)} %copy.377), calls=%async_computation.9 | async-start | bytes 786432 | tf_op jit(solution)/shard_map/all_to_all | solution.py:189
  751.9 137.1 %all-gather.23.cloned.1.call-start = ((), (), s32[]{:S(2)}) async-start(), calls=%async_computation.17 | async-start | bytes 2211840 | tf_op jit(solution)/shard_map/all_gather | solution.py:10
  765.3 4.3 collective-permute-start.6
  771.6 39.7 %copy-start.81 = (pred[80,16]{0,1:T(8,128)(4,1)S(1)}, pred[80,16]{0,1:T(8,128)(4,1)}, u32[]{:S(2)}) copy-start(pred[80,16]{0,1:T(8,128)(4,1)} %fusion.167) | copy-start | bytes 3844
  891.8 16.9 %all-to-all-start.11 = ((bf16[16,5,1536]{2,1,0:T(8,128)(2,1)}), bf16[16,5,1536]{2,1,0:T(8,128)(2,1)S(1)}, u32[]{:S(2)}, u32[]{:S(2)}) async-start(bf16[16,5,1536]{2,1,0:T(8,128)(2,1)} %copy.388), calls=%async_computation.11 | async-start | bytes 786432 | tf_op jit(solution)/shard_map/all_to_all | solution.py:189
  (114 other events, 614.8 us)
Sparse Core Ops, SparseCore 0:
  98.7 62.7 all-gather.12
  248.9 59.6 all-gather.14
  394.1 59.6 all-gather.16
  539.4 59.6 all-gather.18
  684.5 59.6 all-gather.20
  829.3 59.6 all-gather.22
